TPU v7x, 32 devices: a whole 2x2x4 slice. The times are simulated.
32 devices in a mesh: lon: 16 (over z, x, core), lat: 2 (over y).
Axes of the slice: x: 2, y: 2, z: 4, core: 2. Of those that a mesh axis runs over, the one named last changes fastest.
Arguments:
- increment: float32 [4, 512, 2048], P(None, 'lat', 'lon'), may hold values from -6 to 6
- kappa_x: float32 [4, 512, 2048], P(None, 'lat', 'lon'), may hold values from 0.02 to 0.2
- kappa_y: float32 [4, 512, 2048], P(None, 'lat', 'lon'), may hold values from 0.02 to 0.2
- metric_x: float32 [512, 2048], P('lat', 'lon'), may hold values from 0.5 to 1.5
- metric_y: float32 [512, 2048], P('lat', 'lon'), may hold values from 0.5 to 1.5
- cell_area: float32 [512, 2048], P('lat', 'lon'), may hold values from 1 to 2
- sea_mask: int32 [4, 512, 2048], P(None, 'lat', 'lon'), may hold values 0 or 1
- fold_partner: int32 [2048], P('lon'), may hold values from 0 to 2047, as said below
- norm_factor: float32 [4, 512, 2048], P(None, 'lat', 'lon'), may hold values from 0.5 to 36, as said below
Outputs:
- adjoint_out: float32 [4, 512, 2048], P(None, 'lat', 'lon')
Inputs may be any that keep to these rules, and one draw needn't show every extreme that they name: fold_partner[i] = (c - i) mod 2048 for one c, so fold_partner[fold_partner[i]] = i. `norm_factor`: positive factors.
All inputs are finite; a program needn't handle non-finite values. No bound on the sum of `sea_mask` on one device may be relied on, other than what follows from the above.
Results may differ from a plain program's by a relative error of at most 0.00002.
Values sent between devices are 32-bit elements; how exact they have to be, the bound alone decides.
No kernel may reach another device: no remote copies, remote signals or barrier semaphores. Data moves between devices by JAX's collectives and lax.ppermute only.
A program may use at most 384 MiB of HBM per device.

v0:
```python
import functools

import jax
import jax.numpy as jnp
from jax import lax
from jax.experimental import pallas as pl
from jax.experimental.pallas import tpu as pltpu
from jax.sharding import PartitionSpec as P

STEPS = 6
LEV = 4
LANES = 128
SUB = 8
PAIR = LANES // 2
EDGES = LEV // 2
WEST = STEPS
EAST = 4 * STEPS
OWN = 2 * STEPS
PART = 4 * STEPS * EDGES
PLANES = 3 * LEV + 1
ENDS = 3 * EDGES + 1
ALL = PLANES + ENDS
TOP = PLANES * STEPS + 2
LEAD_FLOPS = 10_000_000_000
VMEM_LIMIT = 24 * 1024 * 1024
F32 = jnp.float32


def is_even(axis):
    return lax.rem(lax.axis_index(axis), 2) == 0


def lanes_of(shape):
    return lax.broadcasted_iota(jnp.int32, shape, 1)


def roll(x, shift):
    shift = shift % LANES
    return x if shift == 0 else pltpu.roll(x, shift, 1)


def half_lane(shape):
    return jnp.bitwise_and(lanes_of(shape), PAIR - 1)


def pair_up(low, high, shape):
    return jnp.where(lanes_of(shape) < PAIR, low, high)


def own_ends(low, high):
    shape = low.shape
    at = half_lane(shape)
    west = pair_up(roll(low, WEST), roll(high, PAIR + WEST), shape)
    east = pair_up(roll(low, EAST + OWN), roll(high, PAIR + EAST + OWN), shape)
    out = jnp.where((at >= WEST) & (at < WEST + OWN), west, 0.0)
    return jnp.where((at >= EAST) & (at < EAST + OWN), east, out)


def lead_kernel(out_ref):
    out_ref[...] = jnp.zeros_like(out_ref)


def lead():
    return pl.pallas_call(
        lead_kernel,
        out_specs=pl.BlockSpec(memory_space=pltpu.VMEM),
        out_shape=jax.ShapeDtypeStruct((SUB, LANES), F32),
        compiler_params=pltpu.CompilerParams(vmem_limit_bytes=1024 * 1024),
        cost_estimate=pl.CostEstimate(flops=LEAD_FLOPS, bytes_accessed=32, transcendentals=0),
        name="lead",
    )()


def raw_fields(l, rows, inc, kx, ky, mx, my, mask, r):
    sea = mask[l, rows, :].astype(F32)
    return inc[l, rows, :] * r, kx[l, rows, :] * mx * sea, ky[l, rows, :] * my * sea


def fold_way(partner, way_ref, chip_ref, mirror_ref):
    chips = lax.axis_size("lon") // 2
    lon = lax.axis_index("lon")
    head = jnp.sum(jnp.where(lanes_of((1, LANES)) == 0, partner[...].reshape(1, LANES), 0))
    center = lax.rem(head + lon * LANES, chips * 2 * LANES)
    chip = center // (2 * LANES)
    rest = center - chip * 2 * LANES
    inside = (rest >= STEPS - 1) & (rest <= 2 * LANES - STEPS - 1)
    way_ref[...] = jnp.full((LANES,), jnp.where(inside, chip, chips), jnp.int32)
    chip_ref[...] = jnp.full((LANES,), chip, jnp.int32)
    mirror_ref[...] = jnp.full((LANES,), rest + (2 - lax.rem(lon, 2)) * LANES, jnp.int32)


def pack_kernel(start, partner, inc, kx, ky, mx, my, area, mask, edge_ref, m0_ref, m1_ref, way_ref, chip_ref, mirror_ref, acc_first, acc_last):
    del start
    fold_way(partner, way_ref, chip_ref, mirror_ref)
    rows = inc.shape[1]
    columns = m1_ref.shape[0]
    chunk = 32
    side = 2 * SUB
    even = is_even("lon")
    lane = lanes_of((chunk, LANES))
    for at in range(0, rows, chunk):
        here = pl.ds(at, chunk)
        r = 1.0 / area[here, :]
        mxv, myv = mx[here, :], my[here, :]
        first = jnp.zeros((chunk, LANES), F32)
        last = jnp.zeros((chunk, LANES), F32)
        planes = [None] * PLANES
        planes[3 * LEV] = r
        for l in range(LEV):
            fields = raw_fields(l, here, inc, kx, ky, mxv, myv, mask, r) + (r,)
            planes[l : 3 * LEV : LEV] = fields[:3]
            for p, plane in enumerate(fields):
                lane_at = PAIR * (l % 2) + 4 * STEPS * (l // 2) + STEPS * (p + 1)
                turned = roll(plane, lane_at)
                first = jnp.where((lane >= lane_at) & (lane < lane_at + STEPS), turned, first)
                last = jnp.where((lane >= lane_at - STEPS) & (lane < lane_at), turned, last)
        acc_first[here, :] = first
        acc_last[here, :] = last
        if at == 0:
            m0_ref[pl.ds(columns, 2), :] = jnp.zeros((2, LANES), F32)
            for p in range(PLANES):
                edge_ref[p, side:, :] = planes[p][:side]
        if at == rows - chunk:
            for p in range(PLANES):
                edge_ref[p, :side, :] = planes[p][chunk - side :]
                m0_ref[pl.ds(columns + 2 + STEPS * p, STEPS), :] = planes[p][chunk - STEPS :]
    for i in range(rows // LANES):
        first = jnp.transpose(acc_first[pl.ds(i * LANES, LANES), :])
        last = jnp.transpose(acc_last[pl.ds(i * LANES, LANES), :])
        for q in range(2):
            to = pl.ds((2 * i + q) * PART, PART)
            one = first[PAIR * q + STEPS : PAIR * q + STEPS + PART]
            two = last[PAIR * q : PAIR * q + PART]
            m0_ref[to, :] = jnp.where(even, two, one)
            m1_ref[to, :] = jnp.where(even, one, two)


def pack(start, partner, *fields):
    shape = fields[0].shape
    vm = pl.BlockSpec(memory_space=pltpu.VMEM)
    columns = shape[1] // LANES * 2 * PART
    acc = pltpu.VMEM(shape[1:], F32)
    return pl.pallas_call(
        pack_kernel,
        in_specs=[pl.BlockSpec(memory_space=pl.ANY)] + [vm] * 8,
        out_specs=[vm] * 6,
        out_shape=[jax.ShapeDtypeStruct((PLANES, 4 * SUB, LANES), F32)]
        + [jax.ShapeDtypeStruct((n, LANES), F32) for n in (columns + TOP, columns)]
        + [jax.ShapeDtypeStruct((LANES,), jnp.int32)] * 3,
        scratch_shapes=[acc, acc],
        compiler_params=pltpu.CompilerParams(vmem_limit_bytes=VMEM_LIMIT),
        name="pack",
    )(start, partner, *fields)


def untranspose(msg_ref, half, buf):
    buf[pl.ds(0, PART), :] = msg_ref[pl.ds(2 * PART * half, PART), :]
    buf[pl.ds(PAIR, PART), :] = msg_ref[pl.ds(2 * PART * half + PART, PART), :]
    return jnp.transpose(buf[...])


def halo_half(g0, g1, half, buf):
    t0 = untranspose(g0, half, buf)
    t1 = untranspose(g1, half, buf)
    even = is_even("lon")
    return jnp.where(even, t1, t0), jnp.where(even, t0, t1)


def with_halo(own, west_t, east_t, e, p):
    at = half_lane(own.shape)
    slot = 4 * STEPS * e + STEPS * p
    out = jnp.where(at < WEST, roll(west_t, -slot), own)
    return jnp.where((at >= EAST + OWN) & (at < EAST + OWN + STEPS), roll(east_t, EAST + OWN - slot), out)


def join_kernel(m0, g0, fold_ref):
    at = m0.shape[0] - TOP
    even = is_even("lon")
    own, other = m0[pl.ds(at, TOP), :], g0[pl.ds(at, TOP), :]
    fold_ref[pl.ds(0, TOP), :] = jnp.where(even, own, other)
    fold_ref[pl.ds(TOP, TOP), :] = jnp.where(even, other, own)


def join(m0, g0):
    vm = pl.BlockSpec(memory_space=pltpu.VMEM)
    return pl.pallas_call(
        join_kernel,
        in_specs=[vm, vm],
        out_specs=vm,
        out_shape=jax.ShapeDtypeStruct((2 * TOP, LANES), F32),
        compiler_params=pltpu.CompilerParams(vmem_limit_bytes=VMEM_LIMIT),
        name="join",
    )(m0, g0)


def join_ends_kernel(fold, hedge, out_ref):
    side = hedge.shape[1] // 2
    out_ref[pl.ds(0, 2 * TOP), :] = fold[...]
    for k in range(ENDS):
        out_ref[pl.ds(2 * TOP + SUB * k, SUB), :] = hedge[k, side - SUB : side, :]


def join_ends(fold, hedge):
    vm = pl.BlockSpec(memory_space=pltpu.VMEM)
    return pl.pallas_call(
        join_ends_kernel,
        in_specs=[vm, vm],
        out_specs=vm,
        out_shape=jax.ShapeDtypeStruct((2 * TOP + ENDS * SUB, LANES), F32),
        compiler_params=pltpu.CompilerParams(vmem_limit_bytes=VMEM_LIMIT),
        name="join_ends",
    )(fold, hedge)


def edge_kernel(g0, g1, edge, hedge_ref, *lat_refs):
    rows = edge.shape[1]
    side = rows // 2
    buf = lat_refs[-1]
    buf[...] = jnp.zeros_like(buf)
    turned = []
    for half, lo in ((1, LANES - side), (0, 0)):
        wt, et = halo_half(g0, g1, half, buf)
        turned.append((wt[lo : lo + side], et[lo : lo + side]))
    west_t, east_t = [jnp.concatenate([turned[0][i], turned[1][i]], axis=0) for i in range(2)]

    def to_lat(k, last, first):
        for ref, even_sends, odd_sends in zip(lat_refs[:-1], (last, first), (first, last)):
            ref[k] = jnp.where(is_even("lat"), even_sends, odd_sends)

    for k in range(ENDS):
        p, e = divmod(k, EDGES)
        low, high = (edge[p * LEV + 2 * e], edge[p * LEV + 2 * e + 1]) if p < 3 else (edge[3 * LEV],) * 2
        value = with_halo(own_ends(low, high), west_t, east_t, e, p)
        hedge_ref[k] = value
        to_lat(PLANES + k, value[side - SUB : side], value[side : side + SUB])
    for p in range(PLANES):
        last, first = edge[p, side - SUB : side, :], edge[p, side : side + SUB, :]
        to_lat(p, last, first)


def edge_messages(g0, g1, edge, lats):
    vm = pl.BlockSpec(memory_space=pltpu.VMEM)
    shapes = [(ENDS, edge.shape[1])] + [(ALL, SUB)] * lats
    return pl.pallas_call(
        edge_kernel,
        in_specs=[vm, vm, vm],
        out_specs=[vm] * len(shapes),
        out_shape=[jax.ShapeDtypeStruct(shape + (LANES,), F32) for shape in shapes],
        scratch_shapes=[pltpu.VMEM((LANES, LANES), F32)],
        compiler_params=pltpu.CompilerParams(vmem_limit_bytes=VMEM_LIMIT),
        name="edge",
    )(g0, g1, edge)


def coefficients(x, y, r, c, at, n, coef, weights=None):
    rows, up, down = pl.ds(at, n), pl.ds(at + 1, n), pl.ds(at - 1, n)
    here = x[c, rows, :]
    xe, xw = roll(here, -1), roll(here, 1)
    sea = jnp.where(here > 0, 1.0, 0.0)
    yv, ys = y[c, rows, :], y[c, down, :]
    east = jnp.where(xe > 0, here, 0.0)
    west = xw * sea
    north = jnp.where(x[c, up, :] > 0, yv, 0.0)
    south = ys * sea
    if weights is not None:
        flip, n_own, n_far, s_own, s_far = weights
        sea_s = jnp.where(x[c, down, :] > 0, 1.0, 0.0)
        east = jnp.where(flip, xe * sea, east)
        west = jnp.where(flip, jnp.where(xw > 0, here, 0.0), west)
        north = n_own * north + n_far * (y[c, up, :] * sea)
        south = s_own * south + s_far * (yv * sea_s)
    east, west, north, south = r * east, r * west, r * north, r * south
    coef[0, c, rows, :] = east
    coef[1, c, rows, :] = west
    coef[2, c, rows, :] = north
    coef[3, c, rows, :] = south
    coef[4, c, rows, :] = 1.0 - ((east + west) + (north + south))


def advance(src, dst, coef, c, at, n):
    rows = pl.ds(at, n)
    here = src[c, rows, :]
    lon = coef[0, c, rows, :] * roll(here, -1) + coef[1, c, rows, :] * roll(here, 1)
    lat = coef[2, c, rows, :] * src[c, pl.ds(at + 1, n), :] + coef[3, c, rows, :] * src[c, pl.ds(at - 1, n), :]
    dst[c, rows, :] = coef[4, c, rows, :] * here + (lon + lat)


def run_steps(one, two, coef, count, lo, hi, n):
    def both(_, carry):
        for src, dst in ((one, two), (two, one)):
            for at in range(lo, hi, n):
                for c in range(count):
                    advance(src, dst, coef, c, at, n)
        return carry

    lax.fori_loop(0, STEPS // 2, both, 0)


def clear_pads(refs, count, lo, hi):
    zero = jnp.zeros((SUB, LANES), F32)
    for ref in refs:
        for c in range(count):
            ref[c, pl.ds(lo - SUB, SUB), :] = zero
            ref[c, pl.ds(hi, SUB), :] = zero


def inner_kernel(inc, kx, ky, mx, my, area, mask, out_ref, ends_ref, one, two, xb, yb, rb, coef):
    rows = inc.shape[1]
    n = 16
    lo, hi = SUB, SUB + rows
    clear_pads((one, two, xb, yb), LEV, lo, hi)
    for at in range(0, rows, n):
        here, there = pl.ds(at, n), pl.ds(lo + at, n)
        r = 1.0 / area[here, :]
        rb[here, :] = r
        mxv, myv = mx[here, :], my[here, :]
        fields = [raw_fields(l, here, inc, kx, ky, mxv, myv, mask, r) for l in range(LEV)]
        for l in range(LEV):
            one[l, there, :], xb[l, there, :], yb[l, there, :] = fields[l]
        for e in range(EDGES):
            for p in range(3):
                ends_ref[p * EDGES + e, here, :] = own_ends(fields[2 * e][p], fields[2 * e + 1][p])
        ends_ref[3 * EDGES, here, :] = own_ends(r, r)
    for at in range(lo, hi, n):
        for l in range(LEV):
            coefficients(xb, yb, rb[pl.ds(at - lo, n), :], l, at, n, coef)
    run_steps(one, two, coef, LEV, lo, hi, n)
    for l in range(LEV):
        out_ref[l] = one[l, pl.ds(lo, rows), :]


def inner(*fields):
    shape = fields[0].shape
    rows = shape[1]
    vm = pl.BlockSpec(memory_space=pltpu.VMEM)
    pad = rows + 2 * SUB
    cells = pltpu.VMEM((LEV, pad, LANES), F32)
    return pl.pallas_call(
        inner_kernel,
        in_specs=[vm] * 7,
        out_specs=[vm, vm],
        out_shape=[
            jax.ShapeDtypeStruct(shape, F32),
            jax.ShapeDtypeStruct((ENDS, rows, LANES), F32),
        ],
        scratch_shapes=[
            cells,
            cells,
            cells,
            cells,
            pltpu.VMEM((rows, LANES), F32),
            pltpu.VMEM((5, LEV, pad, LANES), F32),
        ],
        compiler_params=pltpu.CompilerParams(vmem_limit_bytes=VMEM_LIMIT),
        cost_estimate=pl.CostEstimate(flops=12_000_000, bytes_accessed=6_000_000, transcendentals=0),
        name="inner",
    )(*fields)


def merge(own, ends, l):
    lane = lanes_of(own.shape)
    at = PAIR * (l % 2)
    out = jnp.where(lane < STEPS, roll(ends, -(at + WEST)), own)
    return jnp.where(lane >= LANES - STEPS, roll(ends, -(at + EAST + OWN)), out)


def ends_kernel(ends, g0, g1, mid, norm, area, out_ref, scale_ref, one, two, xb, yb, rb, coef, buf):
    rows = mid.shape[1]
    n = 16
    lo, hi = SUB, SUB + rows
    buf[...] = jnp.zeros_like(buf)
    clear_pads((one, two, xb, yb), EDGES, lo, hi)
    for half in range(2):
        wt, et = halo_half(g0, g1, half, buf)
        here, there = pl.ds(half * LANES, LANES), pl.ds(lo + half * LANES, LANES)
        for e in range(EDGES):
            one[e, there, :] = with_halo(ends[e, here, :], wt, et, e, 0)
            xb[e, there, :] = with_halo(ends[EDGES + e, here, :], wt, et, e, 1)
            yb[e, there, :] = with_halo(ends[2 * EDGES + e, here, :], wt, et, e, 2)
        rb[there, :] = with_halo(ends[3 * EDGES, here, :], wt, et, 0, 3)
    for at in range(lo, hi, n):
        for e in range(EDGES):
            coefficients(xb, yb, rb[pl.ds(at, n), :], e, at, n, coef)
    run_steps(one, two, coef, EDGES, lo, hi, n)
    for l in range(LEV):
        scale = norm[l] * area[...]
        out_ref[l] = scale * merge(mid[l], one[l // 2, pl.ds(lo, rows), :], l)
        scale_ref[l, :SUB, :] = scale[rows - SUB :]
        scale_ref[l, SUB:, :] = scale[:SUB]


def lon_ends(ends, g0, g1, mid, norm, area):
    rows = mid.shape[1]
    vm = pl.BlockSpec(memory_space=pltpu.VMEM)
    pad = rows + 2 * SUB
    cells = pltpu.VMEM((EDGES, pad, LANES), F32)
    return pl.pallas_call(
        ends_kernel,
        in_specs=[vm] * 6,
        out_specs=[vm, vm],
        out_shape=[jax.ShapeDtypeStruct(mid.shape, F32), jax.ShapeDtypeStruct((LEV, 2 * SUB, LANES), F32)],
        scratch_shapes=[
            cells,
            cells,
            cells,
            cells,
            pltpu.VMEM((pad, LANES), F32),
            pltpu.VMEM((5, EDGES, pad, LANES), F32),
            pltpu.VMEM((LANES, LANES), F32),
        ],
        compiler_params=pltpu.CompilerParams(vmem_limit_bytes=VMEM_LIMIT),
        cost_estimate=pl.CostEstimate(flops=8_000_000, bytes_accessed=4_000_000, transcendentals=0),
        name="ends",
    )(ends, g0, g1, mid, norm, area)


def gather(x, idx):
    return jnp.take_along_axis(x, idx, axis=1)


def mirrored(near, far, far_ends, center, ext, put):
    shape = (SUB, LANES)
    lane, at = lanes_of(shape), half_lane(shape)
    flip = SUB - 1 - lax.broadcasted_iota(jnp.int32, shape, 0)
    block = center // LANES
    first = lax.rem(center, LANES)
    own_j = first - lane
    own_i = jnp.bitwise_and(own_j, LANES - 1)
    end_j = first - jnp.where(at < EAST, at - WEST, at - EAST + LANES - OWN)
    end_i = jnp.bitwise_and(end_j, LANES - 1)

    def rows(x):
        return jnp.take_along_axis(x, flip, axis=0)

    for at, rows_of in ((1, far), (3, near)):
        for slot in range(2 * ENDS):
            p, l = divmod(slot, LEV)
            for q in range(2):
                ext[at + q, slot] = rows_of(TOP * q + STEPS * (3 * LEV if p == 3 else slot))
    if far_ends:
        for slot in range(2 * ENDS):
            k, q = divmod(slot, 2)
            ext[0, slot] = roll(far(2 * TOP + SUB * k), -(PAIR * q + WEST))
            ext[5, slot] = roll(near(2 * TOP + SUB * k), -(PAIR * q + EAST + OWN))
    for k in range(ENDS):
        p, e = divmod(k, EDGES)
        both = []
        for q in range(2):
            slot = 2 * k + q
            one, two = ext[block + 1, slot], ext[block, slot]
            if p < 3 or q == 0:
                plane = p * LEV + 2 * e + q if p < 3 else 3 * LEV
                put(plane, rows(jnp.where(own_j >= 0, gather(one, own_i), gather(two, own_i))))
            out = jnp.where(end_j >= 0, gather(one, end_i), gather(two, end_i))
            out = jnp.where(end_j >= LANES, gather(ext[block + 2, slot], end_i), out)
            both.append(jnp.where(end_j < -LANES, gather(ext[block - 1, slot], end_i), out))
        put(PLANES + k, rows(pair_up(both[0], both[1], shape)))


def band_kernel(mirror, edge, hedge, scale, body, fa, fb, *rest):
    lats, (out_ref, one, two, xb, yb, rb, coef, ext, res, sem) = rest[:-10], rest[-10:]
    inner_rows = pl.ds(SUB, body.shape[1] - 2 * SUB)
    copies = [pltpu.make_async_copy(body.at[:, inner_rows, :], out_ref.at[:, inner_rows, :], sem.at[2])]
    copies[0].start()
    side = edge.shape[1] // 2
    count = LEV + EDGES
    even = is_even("lon")
    lat_even = is_even("lat")
    is_top = lax.axis_index("lat") == lax.axis_size("lat") - 1
    lo = SUB
    north, south, own = lo + side, lo + side + SUB, lo + side + 2 * SUB
    hi = own + side
    clear_pads((one, two, xb, yb), count, lo, hi)

    def ghost(plane, of_even, of_odd):
        from_even, from_odd = [lats[i][plane] if i < len(lats) else jnp.zeros((SUB, LANES), F32) for i in (of_even, of_odd)]
        return jnp.where(lat_even, from_even, from_odd)

    def place(plane):
        if plane < 3 * LEV:
            return (one, xb, yb)[plane // LEV].at[plane % LEV]
        if plane == 3 * LEV:
            return rb.at[0]
        p, e = divmod(plane - PLANES, EDGES)
        return rb.at[1] if p == 3 else (one, xb, yb)[p].at[LEV + e]

    for plane in range(ALL):
        ref = place(plane)
        mine = edge.at[plane] if plane < PLANES else hedge.at[plane - PLANES]
        ref[pl.ds(lo, side), :] = mine[:side, :]
        ref[pl.ds(own, side), :] = mine[side:, :]
        ref[pl.ds(south, SUB), :] = ghost(plane, 1, 0)

    @pl.when(is_top)
    def _():
        def put(plane, value):
            place(plane)[pl.ds(north, SUB), :] = value

        def near(at):
            return jnp.where(even, fa[pl.ds(at, SUB), :], fb[pl.ds(at, SUB), :])

        def far(at):
            return jnp.where(even, fb[pl.ds(at, SUB), :], fa[pl.ds(at, SUB), :])

        center = jnp.max(mirror[...].reshape(1, LANES))
        mirrored(near, far, fa.shape[0] > 2 * TOP, center, ext, put)

    @pl.when(jnp.logical_not(is_top))
    def _():
        for plane in range(ALL):
            place(plane)[pl.ds(north, SUB), :] = ghost(plane, 0, 1)

    n = hi - lo
    row = lo + lax.broadcasted_iota(jnp.int32, (n, LANES), 0)
    fold = is_top & (row >= north) & (row < south)
    n_far = jnp.where(is_top & (row == north - 1), 0.5, jnp.where(fold, 1.0, 0.0))
    s_far = jnp.where(is_top & (row == north), 0.5, jnp.where(fold, 1.0, 0.0))
    weights = (fold, 1.0 - n_far, n_far, 1.0 - s_far, s_far)
    for c in range(count):
        coefficients(xb, yb, rb[c // LEV, pl.ds(lo, n), :], c, lo, n, coef, weights)
    run_steps(one, two, coef, count, lo, hi, n)
    for l in range(LEV):
        for i, at in enumerate((north - SUB, own)):
            rows = pl.ds(at, SUB)
            value = merge(one[l, rows, :], one[LEV + l // 2, rows, :], l)
            res[i, l] = scale[l, i * SUB : (i + 1) * SUB, :] * value
    rows = out_ref.shape[1]
    copies += [
        pltpu.make_async_copy(res.at[0], out_ref.at[:, pl.ds(rows - SUB, SUB), :], sem.at[0]),
        pltpu.make_async_copy(res.at[1], out_ref.at[:, pl.ds(0, SUB), :], sem.at[1]),
    ]
    for copy in copies[1:]:
        copy.start()
    for copy in copies:
        copy.wait()


def band(mirror, edge, hedge, scale, body, fa, fb, lats):
    vm = pl.BlockSpec(memory_space=pltpu.VMEM)
    anywhere = pl.BlockSpec(memory_space=pl.ANY)
    pad = edge.shape[1] + 4 * SUB
    cells = pltpu.VMEM((LEV + EDGES, pad, LANES), F32)
    return pl.pallas_call(
        band_kernel,
        in_specs=[vm] * (7 + len(lats)),
        out_specs=anywhere,
        out_shape=pltpu.HBM(body.shape, F32),
        scratch_shapes=[
            cells,
            cells,
            cells,
            cells,
            pltpu.VMEM((2, pad, LANES), F32),
            pltpu.VMEM((5, LEV + EDGES, pad, LANES), F32),
            pltpu.VMEM((6, 2 * ENDS, SUB, LANES), F32),
            pltpu.VMEM((2, LEV, SUB, LANES), F32),
            pltpu.SemaphoreType.DMA((3,)),
        ],
        compiler_params=pltpu.CompilerParams(vmem_limit_bytes=VMEM_LIMIT),
        name="band",
    )(mirror, edge, hedge, scale, body, fa, fb, *lats)


def table(axes, sizes, send):
    place = {axis: i for i, axis in enumerate(axes)}

    def flat(lon, lat):
        spot = {"lon": lon, "lat": lat}
        index = 0
        for axis in axes:
            index = index * sizes[axis] + spot[axis]
        return index

    pairs = []
    for lon in range(sizes["lon"]):
        for lat in range(sizes["lat"]):
            to = send(lon, lat)
            if to is not None:
                pairs.append((flat(lon, lat), flat(to[0] % sizes["lon"], to[1])))
    return pairs


def per_device(axes, sizes, inc, kx, ky, mx, my, area, mask, fold_partner, norm):
    n_lon, n_lat = sizes["lon"], sizes["lat"]
    chips = n_lon // 2

    def permute(x, send):
        return lax.ppermute(x, axes, table(axes, sizes, send))

    def sibling(o, a):
        return o + 1 - 2 * (o % 2), a

    def outer(o, a):
        return o - 1 + 2 * (o % 2), a

    def even_lat(o, a):
        return o, a + 1 - 2 * (a % 2)

    def odd_lat(o, a):
        to = a - 1 + 2 * (a % 2)
        return (o, to) if 0 <= to < n_lat else None

    def across(chip):
        def send(o, a):
            if a < n_lat - 1:
                return sibling(o, a)
            return (2 * ((chip - o // 2) % chips), a) if o % 2 else (2 * ((chip - 1 - o // 2) % chips) + 1, a)

        return lambda x: permute(x, send)

    def finish(over_fold):
        def branch(m0, m1, edge, chip, mirror, fields, norm):
            g0 = permute(m0, sibling)
            g1 = permute(m1, outer)
            fold = join(m0, g0)
            if over_fold is not None:
                fa = over_fold(fold)
                fold, fields = lax.optimization_barrier((fold, fields))
            mid, ends = inner(*fields)
            edge, mid = lax.optimization_barrier((edge, mid))
            hedge, *rows = edge_messages(g0, g1, edge, 1 if n_lat == 2 else 2)
            if over_fold is None:
                fa = lax.switch(chip[0], [across(i) for i in range(chips)], join_ends(fold, hedge))
            lats = [permute(x, send) for x, send in zip(rows, (even_lat, odd_lat))]
            body, scale = lon_ends(ends, g0, g1, mid, norm, fields[5])
            fa, scale, lats = lax.optimization_barrier((fa, scale, lats))
            fb = permute(fa, sibling)
            return band(mirror, edge, hedge, scale, body, fa, fb, lats)

        return branch

    fields = (inc, kx, ky, mx, my, area, mask)
    edge, m0, m1, way, chip, mirror = pack(lead(), fold_partner, *fields)
    branches = [finish(across(i)) for i in range(chips)] + [finish(None)]
    return lax.switch(way[0], branches, m0, m1, edge, chip, mirror, fields, norm)


def solution(mesh):
    axes = tuple(mesh.axis_names)
    sizes = dict(mesh.shape)
    cube, flat = P(None, "lat", "lon"), P("lat", "lon")
    return jax.shard_map(
        functools.partial(per_device, axes, sizes),
        mesh=mesh,
        in_specs=(cube, cube, cube, flat, flat, flat, cube, P("lon"), cube),
        out_specs=cube,
        check_vma=False,
    )
```

profile of v0, /device:TPU:0, one launch (start us, length us, event | category | flops | bytes accessed | tf_op | source)
XLA Modules:
  0.0 21.1 jit_solution(12106492481350092547)
XLA Ops:
  0.0 0.0 copy-start.4
  0.0 0.0 copy-start.5
  0.0 0.0 copy-start.10
  0.0 0.0 copy-start.9
  0.0 0.0 copy-start.3
  0.0 0.0 copy-start.2
  0.0 0.0 copy-start.1
  0.0 0.0 copy-start
  0.1 1.0 %copy-done.4 = s32[4,256,128]{2,1,0:T(8,128)S(1)} copy-done((s32[4,256,128]{2,1,0:T(8,128)S(1)}, s32[4,256,128]{2,1,0:T(8,128)}, u32[]{:S(2)}) %copy-start.4) | copy-done | bytes 524312
  1.0 0.0 copy-done.5
  1.1 0.0 copy-done.10
  1.1 0.0 copy-done.9
  1.1 0.2 copy-done.3
  1.3 0.2 copy-done.2
  1.5 0.2 copy-done.1
  1.6 0.0 copy-done
  1.6 0.0 copy-start.6
  1.6 0.7 %pack.1 = (f32[13,32,128]{2,1,0:T(8,128)S(1)}, f32[272,128]{1,0:T(8,128)S(1)}, f32[192,128]{1,0:T(8,128)S(1)}, s32[128]{0:T(128)S(1)}, s32[128]{0:T(128)S(1)}, /*index=5*/s32[128]{0:T(128)S(1)}) custom-call(f32[8,128]{1,0:T(8,128)S(1)} %lead.1.start, s32[128]{0:T(128)S(1)} %copy-done, f32[4,256,128]{2,1,0:T(8,128)S(1)} %copy-done.1, ...), custom_call_target="tpu_custom_call" | custom-call | tf_op jit(solution)/shard_map/pack/pallas_call | solution.py:143
  2.4 0.3 %copy-done.6 = f32[4,256,128]{2,1,0:T(8,128)S(1)} copy-done((f32[4,256,128]{2,1,0:T(8,128)S(1)}, f32[4,256,128]{2,1,0:T(8,128)}, u32[]{:S(2)}) %copy-start.6) | copy-done | bytes 524312
  2.7 18.1 %conditional.2 = (f32[4,256,128]{2,1,0:T(8,128)}) conditional(s32[]{:T(128)} %bitcast.1, (f32[272,128]{1,0:T(8,128)S(1)}, f32[4,256,128]{2,1,0:T(8,128)S(1)}, f32[4,256,128]{2,1,0:T(8,128)S(1)}, f32[4,256,128]{2,1,0:T(8,128)S(1)}, f32[256,128]{1,0:T(8,128)S(1)}, /*index=5*/f32[256,128]{1,0:T(8,128)S(1)}, ...), branch_computations={%region_0.0_spmd, %region_1.0_spmd, %region_2.0_spmd, %region_3.0_... | conditional | flops 20000000 | bytes 16357280 | solution.py:635
  2.7 0.5 %collective-permute-start = (f32[272,128]{1,0:T(8,128)S(1)}, f32[272,128]{1,0:T(8,128)S(1)}, u32[]{:S(2)}, u32[]{:S(2)}) collective-permute-start(f32[272,128]{1,0:T(8,128)S(1)} %get-tuple-element.235.m0), channel_id=1, source_target_pairs={{0,2},{1,3},{2,0},{3,1},{4,6},{5,7},{6,4},{7,5},{8,10},{9,11},{10,... | collective-permute-start | bytes 417800 | tf_op jit(solution)/shard_map/cond/branch_0_fun/ppermute | solution.py:588
  3.1 5.6 %collective-permute-start.1 = (f32[192,128]{1,0:T(8,128)S(1)}, f32[192,128]{1,0:T(8,128)S(1)}, u32[]{:S(2)}, u32[]{:S(2)}) collective-permute-start(f32[192,128]{1,0:T(8,128)S(1)} %get-tuple-element.269), channel_id=1, source_target_pairs={{0,30},{1,31},{2,4},{3,5},{4,2},{5,3},{6,8},{7,9},{8,6},{9,7},{10,... | collective-permute-start | bytes 294920 | tf_op jit(solution)/shard_map/cond/branch_0_fun/ppermute | solution.py:588
  8.8 0.0 collective-permute-done.g0
  8.8 0.1 collective-permute-start.2
  8.9 3.2 %inner.9 = (f32[4,256,128]{2,1,0:T(8,128)S(1)}, f32[7,256,128]{2,1,0:T(8,128)S(1)}) custom-call(f32[4,256,128]{2,1,0:T(8,128)S(1)} %get-tuple-element.260.inc, f32[4,256,128]{2,1,0:T(8,128)S(1)} %get-tuple-element.261.kx, f32[4,256,128]{2,1,0:T(8,128)S(1)} %get-tuple-element.262.ky, f32[256,128]{1,0:T(8,128)S(1)} %get-tuple-element.263.mx, ...), custom_call_target="tpu_custom_call" | custom-call | flops 12000000 | bytes 6000000 | tf_op jit(solution)/shard_map/cond/branch_0_fun/inner/pallas_call | solution.py:338
  12.0 0.0 collective-permute-done.1.g1
  12.0 0.3 %edge.9 = (f32[7,32,128]{2,1,0:T(8,128)S(1)}, f32[20,8,128]{2,1,0:T(8,128)S(1)}) custom-call(f32[272,128]{1,0:T(8,128)S(1)} %collective-permute-done.g0, f32[192,128]{1,0:T(8,128)S(1)} %collective-permute-done.1.g1, f32[13,32,128]{2,1,0:T(8,128)S(1)} %get-tuple-element.268.edge), custom_call_target="tpu_custom_call" | custom-call | tf_op jit(solution)/shard_map/cond/branch_0_fun/edge/pallas_call | solution.py:244
  12.4 2.6 %collective-permute-start.3 = (f32[20,8,128]{2,1,0:T(8,128)S(1)}, f32[20,8,128]{2,1,0:T(8,128)S(1)}, u32[]{:S(2)}, u32[]{:S(2)}) collective-permute-start(f32[20,8,128]{2,1,0:T(8,128)S(1)} %get-tuple-element.275), channel_id=1, source_target_pairs={{0,1},{1,0},{2,3},{3,2},{4,5},{5,4},{6,7},{7,6},{8,9},{9,8},{10,11... | collective-permute-start | bytes 245768 | tf_op jit(solution)/shard_map/cond/branch_0_fun/ppermute | solution.py:588
  14.9 2.1 %ends.9 = (f32[4,256,128]{2,1,0:T(8,128)S(1)}, f32[4,16,128]{2,1,0:T(8,128)S(1)}) custom-call(f32[7,256,128]{2,1,0:T(8,128)S(1)} %get-tuple-element.271.ends, f32[272,128]{1,0:T(8,128)S(1)} %collective-permute-done.g0, f32[192,128]{1,0:T(8,128)S(1)} %collective-permute-done.1.g1, f32[4,256,128]{2,1,0:T(8,128)S(1)} %get-tuple-element.272.mid, ...), custom_call_target="tpu_custom_call" | custom-call | flops 8000000 | bytes 4000000 | tf_op jit(solution)/shard_map/cond/branch_0_fun/ends/pallas_call | solution.py:397
  17.0 0.0 collective-permute-done.2.fa
  17.1 0.3 %collective-permute-done.3.rest_0_ = f32[20,8,128]{2,1,0:T(8,128)S(1)} collective-permute-done((f32[20,8,128]{2,1,0:T(8,128)S(1)}, f32[20,8,128]{2,1,0:T(8,128)S(1)}, u32[]{:S(2)}, u32[]{:S(2)}) %collective-permute-start.3) | collective-permute-done | bytes 81952 | tf_op jit(solution)/shard_map/cond/branch_0_fun/ppermute | solution.py:588
  17.4 0.0 collective-permute-start.4
  17.4 1.3 %collective-permute-done.4.fb = f32[160,128]{1,0:T(8,128)S(1)} collective-permute-done((f32[160,128]{1,0:T(8,128)S(1)}, f32[160,128]{1,0:T(8,128)S(1)}, u32[]{:S(2)}, u32[]{:S(2)}) %collective-permute-start.4) | collective-permute-done | bytes 81952 | tf_op jit(solution)/shard_map/cond/branch_0_fun/ppermute | solution.py:588
  18.6 1.6 %band.9 = f32[4,256,128]{2,1,0:T(8,128)} custom-call(s32[128]{0:T(128)S(1)} %get-tuple-element.231.mirror, f32[13,32,128]{2,1,0:T(8,128)S(1)} %get-tuple-element.268.edge, f32[7,32,128]{2,1,0:T(8,128)S(1)} %get-tuple-element.270.hedge, f32[4,16,128]{2,1,0:T(8,128)S(1)} %get-tuple-element.276.scale, f32[4,256,128]{2,1,0:T(8,128)S(1)} %get-tuple-element.277.body, ...), custom_call_target="tpu_custom_call" | custom-call | tf_op jit(solution)/shard_map/cond/branch_0_fun/band/pallas_call | solution.py:543
  (2 shorter events, 0.0 us)
Async XLA Ops:
  0.0 1.0 %copy-start.4 = (s32[4,256,128]{2,1,0:T(8,128)S(1)}, s32[4,256,128]{2,1,0:T(8,128)}, u32[]{:S(2)}) copy-start(s32[4,256,128]{2,1,0:T(8,128)} %mask.1) | copy-start | bytes 1572868
  0.0 1.1 %copy-start.5 = (f32[256,128]{1,0:T(8,128)S(1)}, f32[256,128]{1,0:T(8,128)}, u32[]{:S(2)}) copy-start(f32[256,128]{1,0:T(8,128)} %area.1) | copy-start | bytes 393220
  0.0 1.1 %copy-start.10 = (f32[256,128]{1,0:T(8,128)S(1)}, f32[256,128]{1,0:T(8,128)}, u32[]{:S(2)}) copy-start(f32[256,128]{1,0:T(8,128)} %my.1) | copy-start | bytes 393220
  0.0 1.1 %copy-start.9 = (f32[256,128]{1,0:T(8,128)S(1)}, f32[256,128]{1,0:T(8,128)}, u32[]{:S(2)}) copy-start(f32[256,128]{1,0:T(8,128)} %mx.1) | copy-start | bytes 393220
  0.0 1.3 %copy-start.3 = (f32[4,256,128]{2,1,0:T(8,128)S(1)}, f32[4,256,128]{2,1,0:T(8,128)}, u32[]{:S(2)}) copy-start(f32[4,256,128]{2,1,0:T(8,128)} %ky.1) | copy-start | bytes 1572868
  0.0 1.5 %copy-start.2 = (f32[4,256,128]{2,1,0:T(8,128)S(1)}, f32[4,256,128]{2,1,0:T(8,128)}, u32[]{:S(2)}) copy-start(f32[4,256,128]{2,1,0:T(8,128)} %kx.1) | copy-start | bytes 1572868
  0.0 1.6 %copy-start.1 = (f32[4,256,128]{2,1,0:T(8,128)S(1)}, f32[4,256,128]{2,1,0:T(8,128)}, u32[]{:S(2)}) copy-start(f32[4,256,128]{2,1,0:T(8,128)} %inc.1) | copy-start | bytes 1572868
  0.0 1.6 %copy-start = (s32[128]{0:T(128)S(1)}, s32[128]{0:T(128)}, u32[]{:S(2)}) copy-start(s32[128]{0:T(128)} %partner.1) | copy-start | bytes 1540
  1.6 1.0 %copy-start.6 = (f32[4,256,128]{2,1,0:T(8,128)S(1)}, f32[4,256,128]{2,1,0:T(8,128)}, u32[]{:S(2)}) copy-start(f32[4,256,128]{2,1,0:T(8,128)} %param.34) | copy-start | bytes 1572868
  2.7 6.1 %collective-permute-start = (f32[272,128]{1,0:T(8,128)S(1)}, f32[272,128]{1,0:T(8,128)S(1)}, u32[]{:S(2)}, u32[]{:S(2)}) collective-permute-start(f32[272,128]{1,0:T(8,128)S(1)} %get-tuple-element.235.m0), channel_id=1, source_target_pairs={{0,2},{1,3},{2,0},{3,1},{4,6},{5,7},{6,4},{7,5},{8,10},{9,11},{10,... | collective-permute-start | bytes 417800 | tf_op jit(solution)/shard_map/cond/branch_0_fun/ppermute | solution.py:588
  3.1 8.9 %collective-permute-start.1 = (f32[192,128]{1,0:T(8,128)S(1)}, f32[192,128]{1,0:T(8,128)S(1)}, u32[]{:S(2)}, u32[]{:S(2)}) collective-permute-start(f32[192,128]{1,0:T(8,128)S(1)} %get-tuple-element.269), channel_id=1, source_target_pairs={{0,30},{1,31},{2,4},{3,5},{4,2},{5,3},{6,8},{7,9},{8,6},{9,7},{10,... | collective-permute-start | bytes 294920 | tf_op jit(solution)/shard_map/cond/branch_0_fun/ppermute | solution.py:588
  8.8 8.2 %collective-permute-start.2 = (f32[160,128]{1,0:T(8,128)S(1)}, f32[160,128]{1,0:T(8,128)S(1)}, u32[]{:S(2)}, u32[]{:S(2)}) collective-permute-start(f32[160,128]{1,0:T(8,128)S(1)} %join.9), channel_id=1, source_target_pairs={{0,2},{1,31},{2,0},{3,1},{4,6},{5,27},{6,4},{7,29},{8,10},{9,23},{... | collective-permute-start | bytes 245768 | tf_op jit(solution)/shard_map/cond/branch_0_fun/ppermute | solution.py:588
  12.4 5.0 %collective-permute-start.3 = (f32[20,8,128]{2,1,0:T(8,128)S(1)}, f32[20,8,128]{2,1,0:T(8,128)S(1)}, u32[]{:S(2)}, u32[]{:S(2)}) collective-permute-start(f32[20,8,128]{2,1,0:T(8,128)S(1)} %get-tuple-element.275), channel_id=1, source_target_pairs={{0,1},{1,0},{2,3},{3,2},{4,5},{5,4},{6,7},{7,6},{8,9},{9,8},{10,11... | collective-permute-start | bytes 245768 | tf_op jit(solution)/shard_map/cond/branch_0_fun/ppermute | solution.py:588
  17.4 1.3 %collective-permute-start.4 = (f32[160,128]{1,0:T(8,128)S(1)}, f32[160,128]{1,0:T(8,128)S(1)}, u32[]{:S(2)}, u32[]{:S(2)}) collective-permute-start(f32[160,128]{1,0:T(8,128)S(1)} %collective-permute-done.2.fa), channel_id=1, source_target_pairs={{0,2},{1,3},{2,0},{3,1},{4,6},{5,7},{6,4},{7,5},{8,10},{9,11},{10,... | collective-permute-start | bytes 245768 | tf_op jit(solution)/shard_map/cond/branch_0_fun/ppermute | solution.py:588
where the time goes:
time: 21.2 us; the launch traced here: 21.1 us
  starting transfers between devices  8.71 us (41%)
  Pallas kernels  7.94 us (37%)
  local copies, waits for them, and re-layouts  1.86 us (9%)
  waiting for transfers between devices  1.58 us (7%)
  loops' own time  0.64 us (3%)
  between operations  0.33 us (2%)
    ppermute x5, starting transfers between devices, permute(): return lax.ppermute(x, axes, table(axes, sizes, send))  8.71 us
    pallas_call x1, Pallas kernels, inner(): pl.pallas_call(inner_kernel, in_specs=[vm] * 7, out_specs=[vm, vm], out_s...  3.16 us
    pallas_call x1, Pallas kernels, lon_ends(): pl.pallas_call(ends_kernel, in_specs=[vm] * 6, out_specs=[vm, vm], out_sh...  2.1 us
    unnamed x18, local copies, waits for them, and re-layouts  1.86 us
    pallas_call x1, Pallas kernels, band(): pl.pallas_call(band_kernel, in_specs=[vm] * (7 + len(lats)), out_specs=an...  1.6 us
    ppermute x5, waiting for transfers between devices, permute(): return lax.ppermute(x, axes, table(axes, sizes, send))  1.58 us
    pallas_call x1, Pallas kernels, pack(): pl.pallas_call(pack_kernel, in_specs=[pl.BlockSpec(memory_space=pl.ANY)]...  0.73 us
    another operation x1, loops' own time, per_device(): lax.switch(way[0], branches, m0, m1, edge, chip, mirror, fields, norm)  0.64 us
  transfers between devices with their start and end apart: 5, of which 2 were waited for; matrix products, arithmetic and copies ran while one was open for 0% of the time, Pallas kernels for 27%

commit v1 on v0

--- a/solution.py
+++ b/solution.py
@@ -21,6 +21,7 @@
 ENDS = 3 * EDGES + 1
 ALL = PLANES + ENDS
 TOP = PLANES * STEPS + 2
+PREP = 4
 LEAD_FLOPS = 10_000_000_000
 VMEM_LIMIT = 24 * 1024 * 1024
 F32 = jnp.float32
@@ -309,8 +310,15 @@
     n = 16
     lo, hi = SUB, SUB + rows
     clear_pads((one, two, xb, yb), LEV, lo, hi)
-    for at in range(0, rows, n):
-        here, there = pl.ds(at, n), pl.ds(lo + at, n)
+    span = rows // PREP
+
+    def prepare(i, carry):
+        for at in range(0, span, n):
+            at = pl.multiple_of(i * span + at, n)
+            prepare_rows(pl.ds(at, n), pl.ds(lo + at, n))
+        return carry
+
+    def prepare_rows(here, there):
         r = 1.0 / area[here, :]
         rb[here, :] = r
         mxv, myv = mx[here, :], my[here, :]
@@ -321,9 +329,15 @@
             for p in range(3):
                 ends_ref[p * EDGES + e, here, :] = own_ends(fields[2 * e][p], fields[2 * e + 1][p])
         ends_ref[3 * EDGES, here, :] = own_ends(r, r)
-    for at in range(lo, hi, n):
-        for l in range(LEV):
-            coefficients(xb, yb, rb[pl.ds(at - lo, n), :], l, at, n, coef)
+    def combine(i, carry):
+        for at in range(0, span, n):
+            at = pl.multiple_of(i * span + at, n)
+            for l in range(LEV):
+                coefficients(xb, yb, rb[pl.ds(at, n), :], l, lo + at, n, coef)
+        return carry
+
+    lax.fori_loop(0, PREP, prepare, 0)
+    lax.fori_loop(0, PREP, combine, 0)
     run_steps(one, two, coef, LEV, lo, hi, n)
     for l in range(LEV):
         out_ref[l] = one[l, pl.ds(lo, rows), :]
@@ -623,7 +637,7 @@
                 fa = lax.switch(chip[0], [across(i) for i in range(chips)], join_ends(fold, hedge))
             lats = [permute(x, send) for x, send in zip(rows, (even_lat, odd_lat))]
             body, scale = lon_ends(ends, g0, g1, mid, norm, fields[5])
-            fa, scale, lats = lax.optimization_barrier((fa, scale, lats))
+            fa, scale = lax.optimization_barrier((fa, scale))
             fb = permute(fa, sibling)
             return band(mirror, edge, hedge, scale, body, fa, fb, lats)
 

time: 21.2 us -> 20.5 us (0.967)
  starting transfers between devices: 8.71 us -> 7.91 us
  Pallas kernels: 7.94 us -> 8.45 us
  waiting for transfers between devices: 1.58 us -> 1.24 us
  loops' own time: 0.64 us -> 0.41 us
    ppermute x5, starting transfers between devices: 8.71 us -> 7.91 us  [permute(): return lax.ppermute(x, axes, table(axes, sizes, send))]
    pallas_call x1, Pallas kernels: 3.16 us -> 3.67 us  [inner(): pl.pallas_call(inner_kernel, in_specs=[vm] * 7, out_specs=[vm, vm], out_s...]
    ppermute x5, waiting for transfers between devices: 1.58 us -> 1.24 us  [permute(): return lax.ppermute(x, axes, table(axes, sizes, send))]
    another operation x1, loops' own time: 0.64 us -> 0.41 us  [per_device(): lax.switch(way[0], branches, m0, m1, edge, chip, mirror, fields, norm)]
  transfers between devices with their start and end apart: 5 -> 5, of which waited for: 2 -> 2; matrix products, arithmetic and copies ran while one was open for 0% -> 0% of each run, Pallas kernels for 27% -> 30%
where the time goes in v1:
time: 20.5 us; the launch traced here: 20.2 us
  Pallas kernels  8.45 us (41%)
  starting transfers between devices  7.91 us (39%)
  local copies, waits for them, and re-layouts  1.86 us (9%)
  waiting for transfers between devices  1.24 us (6%)
  loops' own time  0.41 us (2%)
  between operations  0.33 us (2%)
    ppermute x5, starting transfers between devices, permute(): return lax.ppermute(x, axes, table(axes, sizes, send))  7.91 us
    pallas_call x1, Pallas kernels, inner(): pl.pallas_call(inner_kernel, in_specs=[vm] * 7, out_specs=[vm, vm], out_s...  3.67 us
    pallas_call x1, Pallas kernels, lon_ends(): pl.pallas_call(ends_kernel, in_specs=[vm] * 6, out_specs=[vm, vm], out_sh...  2.1 us
    unnamed x18, local copies, waits for them, and re-layouts  1.86 us
    pallas_call x1, Pallas kernels, band(): pl.pallas_call(band_kernel, in_specs=[vm] * (7 + len(lats)), out_specs=an...  1.6 us
    ppermute x5, waiting for transfers between devices, permute(): return lax.ppermute(x, axes, table(axes, sizes, send))  1.24 us
    pallas_call x1, Pallas kernels, pack(): pl.pallas_call(pack_kernel, in_specs=[pl.BlockSpec(memory_space=pl.ANY)]...  0.73 us
  transfers between devices with their start and end apart: 5, of which 2 were waited for; matrix products, arithmetic and copies ran while one was open for 0% of the time, Pallas kernels for 30%

profile of v1, /device:TPU:0, one launch (start us, length us, event | category | flops | bytes accessed | tf_op | source)
XLA Modules:
  0.0 20.2 jit_solution(16542892902208605795)
XLA Ops:
  0.0 0.0 copy-start.4
  0.0 0.0 copy-start.5
  0.0 0.0 copy-start.10
  0.0 0.0 copy-start.9
  0.0 0.0 copy-start.3
  0.0 0.0 copy-start.2
  0.0 0.0 copy-start.1
  0.0 0.0 copy-start
  0.1 1.0 %copy-done.4 = s32[4,256,128]{2,1,0:T(8,128)S(1)} copy-done((s32[4,256,128]{2,1,0:T(8,128)S(1)}, s32[4,256,128]{2,1,0:T(8,128)}, u32[]{:S(2)}) %copy-start.4) | copy-done | bytes 524312
  1.0 0.0 copy-done.5
  1.1 0.0 copy-done.10
  1.1 0.0 copy-done.9
  1.1 0.2 copy-done.3
  1.3 0.2 copy-done.2
  1.5 0.2 copy-done.1
  1.6 0.0 copy-done
  1.6 0.0 copy-start.6
  1.6 0.7 %pack.1 = (f32[13,32,128]{2,1,0:T(8,128)S(1)}, f32[272,128]{1,0:T(8,128)S(1)}, f32[192,128]{1,0:T(8,128)S(1)}, s32[128]{0:T(128)S(1)}, s32[128]{0:T(128)S(1)}, /*index=5*/s32[128]{0:T(128)S(1)}) custom-call(f32[8,128]{1,0:T(8,128)S(1)} %lead.1.start, s32[128]{0:T(128)S(1)} %copy-done, f32[4,256,128]{2,1,0:T(8,128)S(1)} %copy-done.1, ...), custom_call_target="tpu_custom_call" | custom-call | tf_op jit(solution)/shard_map/pack/pallas_call | solution.py:144
  2.4 0.3 %copy-done.6 = f32[4,256,128]{2,1,0:T(8,128)S(1)} copy-done((f32[4,256,128]{2,1,0:T(8,128)S(1)}, f32[4,256,128]{2,1,0:T(8,128)}, u32[]{:S(2)}) %copy-start.6) | copy-done | bytes 524312
  2.7 17.3 %conditional.2 = (f32[4,256,128]{2,1,0:T(8,128)}) conditional(s32[]{:T(128)} %bitcast.1, (f32[272,128]{1,0:T(8,128)S(1)}, f32[4,256,128]{2,1,0:T(8,128)S(1)}, f32[4,256,128]{2,1,0:T(8,128)S(1)}, f32[4,256,128]{2,1,0:T(8,128)S(1)}, f32[256,128]{1,0:T(8,128)S(1)}, /*index=5*/f32[256,128]{1,0:T(8,128)S(1)}, ...), branch_computations={%region_0.0_spmd, %region_1.0_spmd, %region_2.0_spmd, %region_3.0_... | conditional | flops 20000000 | bytes 16357280 | solution.py:649
  2.7 0.5 %collective-permute-start.25 = (f32[272,128]{1,0:T(8,128)S(1)}, f32[272,128]{1,0:T(8,128)S(1)}, u32[]{:S(2)}, u32[]{:S(2)}) collective-permute-start(f32[272,128]{1,0:T(8,128)S(1)} %get-tuple-element.397.m0), channel_id=1, source_target_pairs={{0,2},{1,3},{2,0},{3,1},{4,6},{5,7},{6,4},{7,5},{8,10},{9,11},{10,... | collective-permute-start | bytes 417800 | tf_op jit(solution)/shard_map/cond/branch_5_fun/ppermute | solution.py:602
  3.2 5.6 %collective-permute-start.26 = (f32[192,128]{1,0:T(8,128)S(1)}, f32[192,128]{1,0:T(8,128)S(1)}, u32[]{:S(2)}, u32[]{:S(2)}) collective-permute-start(f32[192,128]{1,0:T(8,128)S(1)} %get-tuple-element.414), channel_id=1, source_target_pairs={{0,30},{1,31},{2,4},{3,5},{4,2},{5,3},{6,8},{7,9},{8,6},{9,7},{10,... | collective-permute-start | bytes 294920 | tf_op jit(solution)/shard_map/cond/branch_5_fun/ppermute | solution.py:602
  8.9 0.0 collective-permute-done.25.g0
  8.9 0.1 collective-permute-start.27
  8.9 3.7 %inner.14 = (f32[4,256,128]{2,1,0:T(8,128)S(1)}, f32[7,256,128]{2,1,0:T(8,128)S(1)}) custom-call(f32[4,256,128]{2,1,0:T(8,128)S(1)} %get-tuple-element.405.inc, f32[4,256,128]{2,1,0:T(8,128)S(1)} %get-tuple-element.406.kx, f32[4,256,128]{2,1,0:T(8,128)S(1)} %get-tuple-element.407.ky, f32[256,128]{1,0:T(8,128)S(1)} %get-tuple-element.408.mx, ...), custom_call_target="tpu_custom_call" | custom-call | flops 12000000 | bytes 6000000 | tf_op jit(solution)/shard_map/cond/branch_5_fun/inner/pallas_call | solution.py:352
  12.6 0.0 collective-permute-done.26.g1
  12.6 0.3 %edge.14 = (f32[7,32,128]{2,1,0:T(8,128)S(1)}, f32[20,8,128]{2,1,0:T(8,128)S(1)}) custom-call(f32[272,128]{1,0:T(8,128)S(1)} %collective-permute-done.25.g0, f32[192,128]{1,0:T(8,128)S(1)} %collective-permute-done.26.g1, f32[13,32,128]{2,1,0:T(8,128)S(1)} %get-tuple-element.413.edge), custom_call_target="tpu_custom_call" | custom-call | tf_op jit(solution)/shard_map/cond/branch_5_fun/edge/pallas_call | solution.py:245
  12.9 1.6 %collective-permute-start.29 = (f32[20,8,128]{2,1,0:T(8,128)S(1)}, f32[20,8,128]{2,1,0:T(8,128)S(1)}, u32[]{:S(2)}, u32[]{:S(2)}) collective-permute-start(f32[20,8,128]{2,1,0:T(8,128)S(1)} %get-tuple-element.423), channel_id=1, source_target_pairs={{0,1},{1,0},{2,3},{3,2},{4,5},{5,4},{6,7},{7,6},{8,9},{9,8},{10,11... | collective-permute-start | bytes 245768 | tf_op jit(solution)/shard_map/cond/branch_5_fun/ppermute | solution.py:602
  14.5 2.1 %ends.14 = (f32[4,256,128]{2,1,0:T(8,128)S(1)}, f32[4,16,128]{2,1,0:T(8,128)S(1)}) custom-call(f32[7,256,128]{2,1,0:T(8,128)S(1)} %get-tuple-element.416.ends, f32[272,128]{1,0:T(8,128)S(1)} %collective-permute-done.25.g0, f32[192,128]{1,0:T(8,128)S(1)} %collective-permute-done.26.g1, f32[4,256,128]{2,1,0:T(8,128)S(1)} %get-tuple-element.417.mid, ...), custom_call_target="tpu_custom_call" | custom-call | flops 8000000 | bytes 4000000 | tf_op jit(solution)/shard_map/cond/branch_5_fun/ends/pallas_call | solution.py:411
  16.6 0.0 collective-permute-done.27.fa
  16.7 0.1 collective-permute-start.28
  16.8 1.1 %collective-permute-done.29.rest_0_ = f32[20,8,128]{2,1,0:T(8,128)S(1)} collective-permute-done((f32[20,8,128]{2,1,0:T(8,128)S(1)}, f32[20,8,128]{2,1,0:T(8,128)S(1)}, u32[]{:S(2)}, u32[]{:S(2)}) %collective-permute-start.29) | collective-permute-done | bytes 81952 | tf_op jit(solution)/shard_map/cond/branch_5_fun/ppermute | solution.py:602
  17.9 0.1 collective-permute-done.28.fb
  18.0 1.6 %band.14 = f32[4,256,128]{2,1,0:T(8,128)} custom-call(s32[128]{0:T(128)S(1)} %get-tuple-element.395.mirror, f32[13,32,128]{2,1,0:T(8,128)S(1)} %get-tuple-element.413.edge, f32[7,32,128]{2,1,0:T(8,128)S(1)} %get-tuple-element.415.hedge, f32[4,16,128]{2,1,0:T(8,128)S(1)} %get-tuple-element.420.scale, f32[4,256,128]{2,1,0:T(8,128)S(1)} %get-tuple-element.421.body, ...), custom_call_target="tpu_custom_call" | custom-call | tf_op jit(solution)/shard_map/cond/branch_5_fun/band/pallas_call | solution.py:557
  (2 shorter events, 0.0 us)
Async XLA Ops:
  0.0 1.0 %copy-start.4 = (s32[4,256,128]{2,1,0:T(8,128)S(1)}, s32[4,256,128]{2,1,0:T(8,128)}, u32[]{:S(2)}) copy-start(s32[4,256,128]{2,1,0:T(8,128)} %mask.1) | copy-start | bytes 1572868
  0.0 1.1 %copy-start.5 = (f32[256,128]{1,0:T(8,128)S(1)}, f32[256,128]{1,0:T(8,128)}, u32[]{:S(2)}) copy-start(f32[256,128]{1,0:T(8,128)} %area.1) | copy-start | bytes 393220
  0.0 1.1 %copy-start.10 = (f32[256,128]{1,0:T(8,128)S(1)}, f32[256,128]{1,0:T(8,128)}, u32[]{:S(2)}) copy-start(f32[256,128]{1,0:T(8,128)} %my.1) | copy-start | bytes 393220
  0.0 1.1 %copy-start.9 = (f32[256,128]{1,0:T(8,128)S(1)}, f32[256,128]{1,0:T(8,128)}, u32[]{:S(2)}) copy-start(f32[256,128]{1,0:T(8,128)} %mx.1) | copy-start | bytes 393220
  0.0 1.3 %copy-start.3 = (f32[4,256,128]{2,1,0:T(8,128)S(1)}, f32[4,256,128]{2,1,0:T(8,128)}, u32[]{:S(2)}) copy-start(f32[4,256,128]{2,1,0:T(8,128)} %ky.1) | copy-start | bytes 1572868
  0.0 1.5 %copy-start.2 = (f32[4,256,128]{2,1,0:T(8,128)S(1)}, f32[4,256,128]{2,1,0:T(8,128)}, u32[]{:S(2)}) copy-start(f32[4,256,128]{2,1,0:T(8,128)} %kx.1) | copy-start | bytes 1572868
  0.0 1.6 %copy-start.1 = (f32[4,256,128]{2,1,0:T(8,128)S(1)}, f32[4,256,128]{2,1,0:T(8,128)}, u32[]{:S(2)}) copy-start(f32[4,256,128]{2,1,0:T(8,128)} %inc.1) | copy-start | bytes 1572868
  0.0 1.6 %copy-start = (s32[128]{0:T(128)S(1)}, s32[128]{0:T(128)}, u32[]{:S(2)}) copy-start(s32[128]{0:T(128)} %partner.1) | copy-start | bytes 1540
  1.6 1.0 %copy-start.6 = (f32[4,256,128]{2,1,0:T(8,128)S(1)}, f32[4,256,128]{2,1,0:T(8,128)}, u32[]{:S(2)}) copy-start(f32[4,256,128]{2,1,0:T(8,128)} %param.34) | copy-start | bytes 1572868
  2.7 6.2 %collective-permute-start.25 = (f32[272,128]{1,0:T(8,128)S(1)}, f32[272,128]{1,0:T(8,128)S(1)}, u32[]{:S(2)}, u32[]{:S(2)}) collective-permute-start(f32[272,128]{1,0:T(8,128)S(1)} %get-tuple-element.397.m0), channel_id=1, source_target_pairs={{0,2},{1,3},{2,0},{3,1},{4,6},{5,7},{6,4},{7,5},{8,10},{9,11},{10,... | collective-permute-start | bytes 417800 | tf_op jit(solution)/shard_map/cond/branch_5_fun/ppermute | solution.py:602
  3.2 9.4 %collective-permute-start.26 = (f32[192,128]{1,0:T(8,128)S(1)}, f32[192,128]{1,0:T(8,128)S(1)}, u32[]{:S(2)}, u32[]{:S(2)}) collective-permute-start(f32[192,128]{1,0:T(8,128)S(1)} %get-tuple-element.414), channel_id=1, source_target_pairs={{0,30},{1,31},{2,4},{3,5},{4,2},{5,3},{6,8},{7,9},{8,6},{9,7},{10,... | collective-permute-start | bytes 294920 | tf_op jit(solution)/shard_map/cond/branch_5_fun/ppermute | solution.py:602
  8.9 7.8 %collective-permute-start.27 = (f32[160,128]{1,0:T(8,128)S(1)}, f32[160,128]{1,0:T(8,128)S(1)}, u32[]{:S(2)}, u32[]{:S(2)}) collective-permute-start(f32[160,128]{1,0:T(8,128)S(1)} %join.14), channel_id=1, source_target_pairs={{0,2},{1,19},{2,0},{3,21},{4,6},{5,15},{6,4},{7,17},{8,10},{9,11},... | collective-permute-start | bytes 245768 | tf_op jit(solution)/shard_map/cond/branch_5_fun/ppermute | solution.py:602
  12.9 4.9 %collective-permute-start.29 = (f32[20,8,128]{2,1,0:T(8,128)S(1)}, f32[20,8,128]{2,1,0:T(8,128)S(1)}, u32[]{:S(2)}, u32[]{:S(2)}) collective-permute-start(f32[20,8,128]{2,1,0:T(8,128)S(1)} %get-tuple-element.423), channel_id=1, source_target_pairs={{0,1},{1,0},{2,3},{3,2},{4,5},{5,4},{6,7},{7,6},{8,9},{9,8},{10,11... | collective-permute-start | bytes 245768 | tf_op jit(solution)/shard_map/cond/branch_5_fun/ppermute | solution.py:602
  16.7 1.3 %collective-permute-start.28 = (f32[160,128]{1,0:T(8,128)S(1)}, f32[160,128]{1,0:T(8,128)S(1)}, u32[]{:S(2)}, u32[]{:S(2)}) collective-permute-start(f32[160,128]{1,0:T(8,128)S(1)} %collective-permute-done.27.fa), channel_id=1, source_target_pairs={{0,2},{1,3},{2,0},{3,1},{4,6},{5,7},{6,4},{7,5},{8,10},{9,11},{10,... | collective-permute-start | bytes 245768 | tf_op jit(solution)/shard_map/cond/branch_5_fun/ppermute | solution.py:602
